TPU v7x, 32 devices: a whole 2x2x4 slice. The times are simulated.
32 devices in a mesh: ma: 4 (over z), row: 8 (over y, x, core).
Axes of the slice: x: 2, y: 2, z: 4, core: 2. Of those that a mesh axis runs over, the one named last changes fastest.
Arguments:
- spectra: float32 [8, 3, 256, 513, 2], P('row', None, 'ma'), may hold values from -0.3125 to 0.3125
- legendre: bfloat16 [256, 513, 384], P('ma'), may hold values from -0.25 to 0.25
- pair_slots: int32 [256], replicated, may hold values from 0 to 255, each once
- theta_owner: int32 [384], replicated, may hold values from 0 to 383, each once
Outputs:
- flux_grid: bfloat16 [8, 768, 2, 1536], P('row', 'ma')
- flux_spectra: float32 [8, 2, 256, 513, 2], P('row', None, 'ma')
Inputs may be any that keep to these rules, and one draw needn't show every extreme that they name: `pair_slots`: A value p below 256 puts the orders p and 511 - p in that slot; values of 256 or more mark empty slots. `theta_owner`: index d of ma owns the northern rows at positions d * 96 to (d + 1) * 96 - 1 and their mirror rows.
All inputs are finite; a program needn't handle non-finite values.
Results may differ from a plain program's by a relative error of at most 0.0077.
Values may be sent and summed in bfloat16 or wider, within the bound.
A program may use at most 192 MiB of HBM per device.

v0:
```python
import jax
import jax.numpy as jnp
from jax import lax
from jax.sharding import PartitionSpec as P

LMAX = 511
NPHI = 1536
NPAIRS = 256
PACK = 513


HIGH = lax.Precision.HIGHEST


def chebyshev_pair(levels):
    index = jnp.arange(levels, dtype=jnp.int32)
    products = index[:, None] * index[None, :] % (2 * (levels - 1))
    cosines = jnp.cos(jnp.pi * products.astype(jnp.float32) / (levels - 1))
    ends = jnp.where((index == 0) | (index == levels - 1), 0.5, 1.0).astype(jnp.float32)
    analysis = (2.0 / (levels - 1)) ** 0.5 * ends[:, None] * ends[None, :] * cosines
    return (cosines, analysis)


def slot_tables(pairs):
    packed = jnp.arange(PACK, dtype=jnp.int32)[None, :]
    column = pairs[:, None]
    in_use = column < NPAIRS
    low_part = in_use & (packed <= LMAX - column)
    high_part = in_use & (packed > LMAX - column)
    high_sign = 1 - 2 * ((packed + LMAX - column + 1) % 2)
    low_sign = jnp.broadcast_to(1 - 2 * (packed % 2), high_sign.shape)
    slot_masks = jnp.stack([low_part, high_part]).astype(jnp.float32)
    slot_signs = jnp.stack([low_sign, high_sign])
    even_part = slot_masks * (slot_signs > 0)
    odd_part = slot_masks * (slot_signs < 0)
    select = jnp.stack([even_part, odd_part], axis=1)
    orders = jnp.stack([pairs, LMAX - pairs], axis=1)
    return (select, orders)


def fourier_tables(orders):
    points = jnp.arange(NPHI, dtype=jnp.int32)
    phase = orders[:, :, None] * points[None, None, :] % NPHI
    angles = 2.0 * jnp.pi * phase.astype(jnp.float32) / NPHI
    analysis_tab = jnp.stack(
        [jnp.cos(angles).astype(jnp.bfloat16), (-jnp.sin(angles)).astype(jnp.bfloat16)]
    )
    weight = jnp.where(orders == 0, 1.0, 2.0).astype(jnp.bfloat16)[None, :, :, None]
    synth_tab = analysis_tab * weight
    return (synth_tab, analysis_tab)


def radial_mix(flattened, matrix):
    lev_dev, columns = flattened.shape
    row_size = lax.axis_size("row")
    block_width = -(-columns // row_size)
    padded = jnp.pad(flattened, ((0, 0), (0, block_width * row_size - columns)))
    blocks = padded.reshape(lev_dev, row_size, block_width)
    combined = jnp.einsum(
        "ab,bxk->axk",
        matrix,
        lax.all_to_all(blocks, "row", split_axis=1, concat_axis=0, tiled=True),
        precision=HIGH,
    )
    result = lax.all_to_all(combined, "row", split_axis=0, concat_axis=1, tiled=True)
    return result.reshape(lev_dev, block_width * row_size)[:, :columns]


def local(spectra, legendre, pair_slots, theta_owner):
    lev_dev = spectra.shape[0]
    slot_dev = spectra.shape[2]
    ma_size = lax.axis_size("ma")
    row_size = lax.axis_size("row")
    half_rows = legendre.shape[2]
    theta_rows = 2 * half_rows
    theta_dev = theta_rows // ma_size
    own_half = theta_dev // 2
    synth_mat, analysis_mat = chebyshev_pair(lev_dev * row_size)
    select, orders = slot_tables(pair_slots)
    synth_tab, analysis_tab = fourier_tables(orders)
    synth_tab = synth_tab.reshape(2, ma_size, slot_dev, 2, NPHI)
    analysis_tab = analysis_tab.reshape(2, ma_size, slot_dev, 2, NPHI)
    select_local = lax.dynamic_slice_in_dim(select, lax.axis_index("ma") * slot_dev, slot_dev, 2)
    select_slots = jnp.transpose(select_local, (2, 0, 1, 3))
    level_sums = radial_mix(spectra.reshape(lev_dev, -1), synth_mat).reshape(spectra.shape)
    level_coeffs = level_sums.astype(jnp.bfloat16)
    spread = jnp.transpose(level_coeffs, (2, 0, 1, 4, 3))
    select_half = select_slots.astype(jnp.bfloat16)
    weighted = spread[:, :, :, :, None, None, :] * select_half[:, None, None, None, :, :, :]
    halves = jnp.einsum(
        "skfcvej,sji->skfcvei", weighted, legendre, preferred_element_type=jnp.float32
    )
    north_rows = (halves[:, :, :, :, :, 0] + halves[:, :, :, :, :, 1]).astype(jnp.bfloat16)
    south_rows = (halves[:, :, :, :, :, 0] - halves[:, :, :, :, :, 1]).astype(jnp.bfloat16)

    def to_owner(values):
        return values[..., theta_owner].reshape(values.shape[:-1] + (ma_size, own_half))

    rows = jnp.stack([to_owner(north_rows), to_owner(south_rows)], axis=-2)
    rows = rows.reshape(north_rows.shape[:-1] + (theta_rows,))
    outgoing = jnp.transpose(rows, (5, 1, 2, 3, 0, 4)).reshape(theta_rows, lev_dev, -1)
    received = lax.all_to_all(outgoing, "ma", split_axis=0, concat_axis=2, tiled=True)
    level_count = received.shape[1]
    spread_in = received.reshape(theta_dev, level_count, ma_size, 3, 2, slot_dev, 2)
    grid_vals = jnp.einsum(
        "tidfcsv,cdsvp->itfp", spread_in, synth_tab, preferred_element_type=jnp.float32
    )
    flux_vals = (grid_vals[:, :, 0:1] * grid_vals[:, :, 1:3]).astype(jnp.bfloat16)
    fourier = jnp.einsum(
        "itgp,cdsvp->itdgcsv", flux_vals, analysis_tab, preferred_element_type=jnp.float32
    ) * NPHI ** (-0.5)
    flux_grid, fourier = (flux_vals, fourier.reshape(level_count, theta_dev, -1))
    fourier = radial_mix(fourier.reshape(lev_dev, -1), analysis_mat).reshape(fourier.shape)
    returned = lax.all_to_all(fourier, "ma", split_axis=2, concat_axis=1, tiled=True)
    split_rows = returned.reshape(lev_dev, ma_size, 2, own_half, 2, 2, slot_dev, 2)
    north_own = split_rows[:, :, 0].reshape(lev_dev, half_rows, 2, 2, slot_dev, 2)
    south_own = split_rows[:, :, 1].reshape(lev_dev, half_rows, 2, 2, slot_dev, 2)
    inverse = (
        jnp.zeros(half_rows, jnp.int32).at[theta_owner].set(jnp.arange(half_rows, dtype=jnp.int32))
    )
    north_nat = jnp.take(north_own, inverse, axis=1)
    south_nat = jnp.take(south_own, inverse, axis=1)
    parity_sums = jnp.stack([north_nat + south_nat, north_nat - south_nat], axis=2)
    by_slot = jnp.transpose(parity_sums, (5, 1, 0, 2, 3, 4, 6))
    flat_values = by_slot.reshape(slot_dev, half_rows, -1)
    upper_part = flat_values.astype(jnp.bfloat16)
    lower_part = (flat_values - upper_part.astype(jnp.float32)).astype(jnp.bfloat16)
    product = jnp.einsum("sji,sir->sjr", legendre, upper_part, preferred_element_type=jnp.float32)
    product = product + jnp.einsum(
        "sji,sir->sjr", legendre, lower_part, preferred_element_type=jnp.float32
    )
    product = product.reshape((slot_dev, legendre.shape[1]) + by_slot.shape[2:])
    spectral = jnp.einsum("sjkegcv,svej->kgsjc", product, select_slots, precision=HIGH)
    return (flux_grid, spectral)


def solution(mesh):
    in_specs = (P("row", None, "ma", None, None), P("ma", None, None), P(), P())
    out_specs = (P("row", "ma", None, None), P("row", None, "ma", None, None))
    return jax.shard_map(local, mesh=mesh, in_specs=in_specs, out_specs=out_specs, check_vma=False)
```

profile of v0, /device:TPU:0, one launch (start us, length us, event | category | flops | bytes accessed | tf_op | source)
XLA Modules:
  0.0 753.1 jit_solution(2241698449954941956)
XLA Ops:
  0.6 25.7 %copy.64 = f32[1,3,64,513,2]{4,3,2,1,0:T(8,128)} copy(f32[1,3,64,513,2]{3,4,2,1,0:T(2,128)} %param.6) | data formatting | bytes 1575936 | tf_op args[0]
  26.3 54.1 %reshape.710 = f32[1,8,24624]{2,0,1:T(1,128)} reshape(f32[1,3,64,513,2]{4,3,2,1,0:T(8,128)} %copy.64) | data formatting | bytes 1575936 | tf_op jit(solution)/shard_map/reshape | solution.py:58
  80.4 5.3 all-to-all-start
  86.8 11.6 %all-to-all-done = f32[1,8,24624]{2,0,1:T(1,128)S(1)} async-done(((f32[1,8,24624]{2,0,1:T(1,128)}), f32[1,8,24624]{2,0,1:T(1,128)S(1)}, u32[]{:S(2)}, u32[]{:S(2)}) %all-to-all-start) | async-done | bytes 788000 | tf_op jit(solution)/shard_map/all_to_all | solution.py:62
  108.7 7.2 all-to-all-done.1
  121.9 45.0 %convert_element_type.140 = bf16[1,3,64,513,2]{4,3,2,1,0:T(8,128)(2,1)} reshape(bf16[8,24624]{1,0:T(8,128)(2,1)} %convert_reduce_fusion) | data formatting | bytes 787968 | tf_op jit(solution)/shard_map/convert_element_type | solution.py:86
  166.8 22.8 %copy.67 = bf16[64,3,2,513]{3,1,2,0:T(4,128)(2,1)S(1)} copy(bf16[64,3,2,513]{2,3,0,1:T(8,128)(2,1)} %bitcast.130) | data formatting | bytes 787968 | tf_op jit(solution)/shard_map/mul | solution.py:89
  189.7 32.6 %fusion.17 = f32[64,1,3,2,2,2,384]{6,2,5,4,3,0,1:T(4,128)} fusion(bf16[64,513,384,1,1,1]{2,0,1,5,4,3:T(8,128)(2,1)} %bitcast.129, bf16[64,2,2,513]{3,2,1,0:T(2,128)(2,1)} %copy.70, bf16[64,3,2,513]{3,1,2,0:T(4,128)(2,1)S(1)} %copy.67), kind=kOutput, calls=%fused_computation.38 | convolution fusion | flops 608311296 | bytes 28230912 | tf_op jit(solution)/shard_map/skfcvej,sji->skfcvei/dot_general | solution.py:90
  225.6 4.9 copy.72
  230.5 6.3 gather_fusion
  244.5 6.3 gather_fusion.1
  250.8 4.9 copy.111
  261.8 5.7 reshape.629
  289.1 15.3 %cosine_convert_fusion = (bf16[1,4,64,2,1536]{4,2,3,1,0:T(8,128)(2,1)}, bf16[1,4,64,2,1536]{4,2,3,1,0:T(8,128)(2,1)}) fusion(s32[4,64,2]{1,2,0:T(2,128)S(1)} %pad_add_fusion.2), kind=kLoop, calls=%fused_computation.24 | loop fusion | flops 9437184 | bytes 3147776 | tf_op jit(solution)/shard_map/convert_element_type | solution.py:46
  304.5 11.5 %all-to-all-done.2 = bf16[4,2,73728]{2,1,0:T(2,128)(2,1)} async-done(((bf16[4,2,73728]{2,1,0:T(2,128)(2,1)}), bf16[4,2,73728]{2,1,0:T(2,128)(2,1)}, u32[]{:S(2)}, u32[]{:S(2)}) %all-to-all-start.2) | async-done | bytes 1179680 | tf_op jit(solution)/shard_map/all_to_all | solution.py:102
  336.5 51.5 %copy.81 = f32[1,192,4,2,2,64,2]{6,5,4,3,2,1,0:T(8,128)} copy(f32[1,192,4,2,2,64,2]{1,5,3,6,2,4,0:T(8,128)} %multiply_bitcast_fusion) | data formatting | bytes 3145728 | tf_op jit(solution)/shard_map/mul | solution.py:109
  388.1 140.0 %reshape.711 = f32[1,8,49152]{2,0,1:T(1,128)} reshape(f32[1,192,4,2,2,64,2]{6,5,4,3,2,1,0:T(8,128)} %copy.81) | data formatting | bytes 3145728 | tf_op jit(solution)/shard_map/reshape | solution.py:58
  532.4 21.0 %all-to-all-done.3 = f32[1,8,49152]{2,0,1:T(1,128)} async-done(((f32[1,8,49152]{2,0,1:T(1,128)}), f32[1,8,49152]{2,0,1:T(1,128)}, u32[]{:S(2)}, u32[]{:S(2)}) %all-to-all-start.3) | async-done | bytes 1572896 | tf_op jit(solution)/shard_map/all_to_all | solution.py:62
  558.6 24.1 %all_to_all.66 = f32[8,1,49152]{2,1,0:T(1,128)} all-to-all(f32[8,1,49152]{2,1,0:T(1,128)S(1)} %copy.83), channel_id=1, replica_groups=mesh['ma'=4,'row'=8] {'row'}, dimensions={0} | all-to-all | bytes 3145728 | tf_op jit(solution)/shard_map/all_to_all | solution.py:65
  582.7 6.3 reduce.2
  591.9 6.0 copy.84
  608.9 41.3 %all-to-all-done.5 = f32[1,192,2048]{1,0,2:T(1,128)} async-done(((f32[1,192,2048]{1,0,2:T(1,128)}), f32[1,192,2048]{1,0,2:T(1,128)}, u32[]{:S(2)}, u32[]{:S(2)}) %all-to-all-start.5) | async-done | bytes 1572896 | tf_op jit(solution)/shard_map/all_to_all | solution.py:114
  684.3 30.1 %fusion.2 = f32[64,16,513]{2,1,0:T(8,128)} fusion(bf16[64,513,384]{2,0,1:T(8,128)(2,1)} %param.7, f32[64,384,16]{1,2,0:T(8,128)S(1)} %reshape.636), kind=kOutput, calls=%fused_computation.9 | convolution fusion | flops 405012480 | bytes 28889088 | tf_op jit(solution)/shard_map/sji,sir->sjr/dot_general | solution.py:129
  714.4 31.2 %add_bitcast_fusion = f32[64,513,16]{1,2,0:T(8,128)} fusion(f32[64,16,513]{2,1,0:T(8,128)} %fusion.2, bf16[64,513,384]{2,0,1:T(8,128)(2,1)} %param.7, f32[64,384,16]{1,2,0:T(8,128)S(1)} %reshape.636), kind=kOutput, calls=%fused_computation.32 | convolution fusion | flops 404358144 | bytes 30990336 | tf_op jit(solution)/shard_map/sji,sir->sjr/dot_general | solution.py:128
  (85 shorter events, 141.3 us)
Async XLA Ops:
  80.4 5.3 copy-start.6
  80.4 17.9 %all-to-all-start = ((f32[1,8,24624]{2,0,1:T(1,128)}), f32[1,8,24624]{2,0,1:T(1,128)S(1)}, u32[]{:S(2)}, u32[]{:S(2)}) async-start(f32[1,8,24624]{2,0,1:T(1,128)} %reshape.710), calls=%async_computation | async-start | bytes 1581056 | tf_op jit(solution)/shard_map/all_to_all | solution.py:62
  103.5 12.5 %all-to-all-start.1 = ((bf16[8,2,12312]{2,1,0:T(2,128)(2,1)}), bf16[8,2,12312]{2,1,0:T(2,128)(2,1)}, u32[]{:S(2)}, u32[]{:S(2)}) async-start(bf16[8,2,12312]{2,1,0:T(2,128)(2,1)} %reshape.716), calls=%async_computation.1 | async-start | bytes 794624 | tf_op jit(solution)/shard_map/all_to_all | solution.py:65
  107.6 1.1 copy-start.7
  244.5 11.3 %copy-start.2 = (bf16[64,1,3,2,2,4,1,96]{7,5,0,4,3,2,6,1:T(4,128)(2,1)S(1)}, bf16[64,1,3,2,2,4,1,96]{7,5,0,4,3,2,6,1:T(4,128)(2,1)}, u32[]{:S(2)}) copy-start(bf16[64,1,3,2,2,4,1,96]{7,5,0,4,3,2,6,1:T(4,128)(2,1)} %copy.110) | copy-start | bytes 1769476
  284.1 31.8 %all-to-all-start.2 = ((bf16[4,2,73728]{2,1,0:T(2,128)(2,1)}), bf16[4,2,73728]{2,1,0:T(2,128)(2,1)}, u32[]{:S(2)}, u32[]{:S(2)}) async-start(bf16[4,2,73728]{2,1,0:T(2,128)(2,1)} %reshape.718), calls=%async_computation.2 | async-start | bytes 2359296 | tf_op jit(solution)/shard_map/all_to_all | solution.py:102
  331.1 1.6 copy-start.4
  331.2 2.3 copy-start.5
  331.5 1.0 copy-start
  528.0 25.3 %all-to-all-start.3 = ((f32[1,8,49152]{2,0,1:T(1,128)}), f32[1,8,49152]{2,0,1:T(1,128)}, u32[]{:S(2)}, u32[]{:S(2)}) async-start(f32[1,8,49152]{2,0,1:T(1,128)} %reshape.711), calls=%async_computation.3 | async-start | bytes 3145728 | tf_op jit(solution)/shard_map/all_to_all | solution.py:62
  597.8 52.3 %all-to-all-start.5 = ((f32[1,192,2048]{1,0,2:T(1,128)}), f32[1,192,2048]{1,0,2:T(1,128)}, u32[]{:S(2)}, u32[]{:S(2)}) async-start(f32[1,192,2048]{1,0,2:T(1,128)} %copy.84), calls=%async_computation.5 | async-start | bytes 4194304 | tf_op jit(solution)/shard_map/all_to_all | solution.py:114
  605.2 1.4 copy-start.1
  745.5 3.3 copy-start.3
where the time goes:
time: 763 us; the launch traced here: 753 us
  local copies, waits for them, and re-layouts  464 us (61%)
  matrix products  107 us (14%)
  waiting for transfers between devices  92.6 us (12%)
  other arithmetic  41.1 us (5%)
  blocking collectives  24.1 us (3%)
  starting transfers between devices  23 us (3%)
    reshape x2, local copies, waits for them, and re-layouts, radial_mix(): blocks = padded.reshape(lev_dev, row_size, block_width)  194 us
    mul x1, local copies, waits for them, and re-layouts, local(): jnp.einsum('itgp,cdsvp->itdgcsv', flux_vals, analysis_tab, preferred_elem...  51.5 us
    unnamed x25, local copies, waits for them, and re-layouts  48.1 us
    convert_element_type x2, local copies, waits for them, and re-layouts, local(): level_coeffs = level_sums.astype(jnp.bfloat16)  47.9 us
    all_to_all x1, waiting for transfers between devices, local(): lax.all_to_all(fourier, 'ma', split_axis=2, concat_axis=1, tiled=True)  41.3 us
    dot_general x1, matrix products, local(): jnp.einsum('skfcvej,sji->skfcvei', weighted, legendre, preferred_element_...  32.6 us
    all_to_all x2, waiting for transfers between devices, radial_mix(): lax.all_to_all(blocks, 'row', split_axis=1, concat_axis=0, tiled=True)  32.6 us
    dot_general x1, matrix products, local(): jnp.einsum('sji,sir->sjr', legendre, upper_part, preferred_element_type=j...  31.2 us
  transfers between devices with their start and end apart: 5, of which 5 were waited for; matrix products, arithmetic and copies ran while one was open for 3% of the time, Pallas kernels for 0%

commit v1 on v0

v1 whole, which is shorter than its diff:
```python
import jax
import jax.numpy as jnp
from jax import lax
from jax.sharding import PartitionSpec as P

LMAX = 511
NPHI = 1536
NPAIRS = 256
PACK = 513
LANES = 128

HIGH = lax.Precision.HIGHEST
BF16 = jnp.bfloat16
F32 = jnp.float32


def chebyshev_pair(levels):
    index = jnp.arange(levels, dtype=jnp.int32)
    products = index[:, None] * index[None, :] % (2 * (levels - 1))
    cosines = jnp.cos(jnp.pi * products.astype(F32) / (levels - 1))
    ends = jnp.where((index == 0) | (index == levels - 1), 0.5, 1.0).astype(F32)
    analysis = (2.0 / (levels - 1)) ** 0.5 * ends[:, None] * ends[None, :] * cosines
    return (cosines, analysis)


def slot_weights(pairs):
    packed = jnp.arange(PACK, dtype=jnp.int32)[None, :]
    column = pairs[:, None]
    in_use = column < NPAIRS
    low = (in_use & (packed <= LMAX - column)).astype(F32)
    high = (in_use & (packed > LMAX - column)).astype(F32)
    low_sign = (1 - 2 * (packed % 2)).astype(F32)
    high_sign = (1 - 2 * ((packed + LMAX - column + 1) % 2)).astype(F32)
    return jnp.stack(
        [jnp.stack([low, low * low_sign], 1), jnp.stack([high, high * high_sign], 1)], 1
    )


def fourier_table(orders):
    points = jnp.arange(NPHI, dtype=jnp.int32)
    phase = orders[:, None, :, None] * points % NPHI
    angles = 2.0 * jnp.pi * phase.astype(F32) / NPHI
    return jnp.concatenate([jnp.cos(angles), -jnp.sin(angles)], axis=1).astype(BF16)


def local(spectra, legendre, pair_slots, theta_owner):
    lev, fields, slots, _, _ = spectra.shape
    ma, row = lax.axis_size("ma"), lax.axis_size("row")
    levels = lev * row
    half = legendre.shape[2]
    own = half // ma
    width = -(-own // LANES) * LANES
    share = -(-slots // row)
    extra = share * row - slots
    devices = ma * row
    synth_mat, analysis_mat = chebyshev_pair(levels)
    place = lax.axis_index("row")

    pairs = jnp.pad(pair_slots.reshape(ma, slots), ((0, 0), (0, extra)), constant_values=NPAIRS)
    mine = pairs.reshape(devices, share)[lax.axis_index("ma") * row + place]
    weights = slot_weights(mine)
    orders = jnp.stack([mine, LMAX - mine], axis=1)
    double = jnp.where(orders == 0, 1.0, 2.0).astype(F32)
    synth_weights = weights * double[:, :, None, None]

    every = pairs.reshape(devices * share)
    table = fourier_table(jnp.stack([every, LMAX - every], axis=1))
    table = table.reshape(devices, share * 4, NPHI)

    if extra:
        chosen = jnp.minimum(place * share + jnp.arange(share), slots - 1)
        functions = jnp.take(legendre, chosen, axis=0)
    else:
        functions = lax.dynamic_slice_in_dim(legendre, place * share, share, 0)
    owners = jnp.pad(
        theta_owner.reshape(ma, own), ((0, 0), (0, width - own)), constant_values=-1
    ).reshape(-1)
    order_rows = (jnp.arange(half)[:, None] == owners[None, :]).astype(BF16)
    functions = jnp.einsum(
        "sji,io->sjo", functions, order_rows, preferred_element_type=F32
    ).astype(BF16)

    outgoing = jnp.transpose(spectra, (2, 0, 1, 4, 3)).astype(BF16)
    outgoing = jnp.pad(outgoing, ((0, extra),) + ((0, 0),) * 4)
    incoming = lax.all_to_all(outgoing, "row", split_axis=0, concat_axis=0, tiled=True)
    incoming = incoming.reshape(row, share, lev, fields, 2, PACK).astype(F32)
    level_coeffs = jnp.einsum(
        "kzl,zslfcj->ksfcj", synth_mat.reshape(levels, row, lev), incoming, precision=HIGH
    ).astype(BF16)

    spread = jnp.transpose(level_coeffs, (1, 0, 2, 3, 4))[:, :, :, None, :, None, :]
    sel = jnp.transpose(synth_weights, (0, 2, 1, 3)).astype(BF16)[:, None, None, :, None, :, :]
    weighted = (spread * sel).reshape(share, levels * fields * 8, PACK)
    north_south = jnp.einsum(
        "smj,sjo->smo", weighted, functions, preferred_element_type=F32
    ).astype(BF16)
    north_south = north_south.reshape(share, row, lev, fields, 2, 4, ma, width)
    to_rows = jnp.transpose(north_south, (6, 1, 2, 3, 4, 0, 5, 7))
    to_rows = to_rows.reshape(devices, lev, fields, 2, share * 4, width)
    at_rows = lax.all_to_all(to_rows, ("ma", "row"), split_axis=0, concat_axis=0, tiled=True)

    grid = jnp.einsum("zlfhnr,znq->lfhrq", at_rows, table, preferred_element_type=F32)
    flux = (grid[:, 0:1] * grid[:, 1:3]).astype(BF16)
    fourier = jnp.einsum("znq,lghrq->zlghnr", table, flux, preferred_element_type=F32)
    fourier = (fourier * NPHI ** (-0.5)).astype(BF16)
    flux_grid = jnp.transpose(flux[:, :, :, :own], (0, 2, 3, 1, 4)).reshape(lev, 2 * own, 2, NPHI)
    back = lax.all_to_all(fourier, ("ma", "row"), split_axis=0, concat_axis=0, tiled=True)

    back = back.reshape(ma, row, lev, 2, 2, share, 2, 2, width)
    back = jnp.transpose(back, (0, 5, 7, 4, 1, 2, 3, 6, 8))
    back = back.reshape(ma, share, 4 * levels * 4, width)
    values = jnp.concatenate([back[d] for d in range(ma)], axis=-1)
    product = jnp.einsum("smo,sjo->smj", values, functions, preferred_element_type=F32)
    product = product.reshape(share, 4, levels * 4, PACK)
    spectral = jnp.sum(product * weights.reshape(share, 4, 1, PACK), axis=1)

    mix = jnp.kron(analysis_mat, jnp.eye(4, dtype=F32))
    mixed = jnp.einsum("nk,skj->nsj", mix, spectral, precision=HIGH).astype(BF16)
    mixed = mixed.reshape(row, lev, 2, 2, share, PACK)
    mixed = jnp.transpose(mixed, (0, 1, 2, 4, 3, 5))
    result = lax.all_to_all(mixed, "row", split_axis=0, concat_axis=0, tiled=True)
    result = jnp.transpose(result, (1, 2, 0, 3, 4, 5)).reshape(lev, 2, row * share, 2, PACK)
    flux_spectra = jnp.transpose(result[:, :, :slots], (0, 1, 2, 4, 3)).astype(F32)
    return (flux_grid, flux_spectra)


def solution(mesh):
    in_specs = (P("row", None, "ma", None, None), P("ma", None, None), P(), P())
    out_specs = (P("row", "ma", None, None), P("row", None, "ma", None, None))
    return jax.shard_map(local, mesh=mesh, in_specs=in_specs, out_specs=out_specs, check_vma=False)
```

time: 763 us -> 136 us (0.18); the launches traced: 753 us -> 135 us
  local copies, waits for them, and re-layouts: 464 us -> 29.4 us
  matrix products: 107 us -> 22.5 us
  waiting for transfers between devices: 92.6 us -> 47 us
  blocking collectives: 24.1 us -> 0 us
  other arithmetic: 41.1 us -> 17.1 us
    reshape x6, local copies, waits for them, and re-layouts: 209 us -> 4.06 us  [the longest x2 1.09 us: local(): mixed = mixed.reshape(row, lev, 2, 2, share, PACK)]
    dot_general x7, matrix products: 107 us -> 22.5 us  [the longest x1 6.91 us: local(): jnp.einsum('zlfhnr,znq->lfhrq', at_rows, table, preferred_element_type=F32)]
    mul x3 -> x4, local copies, waits for them, and re-layouts: 74.4 us -> 2.96 us  [the longest x1 2.73 us: local(): weighted = (spread * sel).reshape(share, levels * fields * 8, PACK)]
    convert_element_type x5 -> x7, local copies, waits for them, and re-layouts: 56.8 us -> 11.1 us  [the longest x3 8.69 us: fourier_table(): jnp.concatenate([jnp.cos(angles), -jnp.sin(angles)], axis=1).astype(BF16)]
    all_to_all x5 -> x4, waiting for transfers between devices: 92.6 us -> 47 us  [the longest x1 25.9 us: local(): lax.all_to_all(fourier, ('ma', 'row'), split_axis=0, concat_axis=0, tiled...]
    unnamed x25 -> x6, local copies, waits for them, and re-layouts: 48.1 us -> 5.89 us
    another operation x11 -> x0, local copies, waits for them, and re-layouts: 33.6 us -> none  [the longest x3 13.3 us: local(): rows = jnp.stack([to_owner(north_rows), to_owner(south_rows)], axis=-2)]
    all_to_all x1 -> x0, blocking collectives: 24.1 us -> none  [radial_mix(): lax.all_to_all(combined, 'row', split_axis=0, concat_axis=1, tiled=True)]
  transfers between devices with their start and end apart: 5 -> 4, of which waited for: 5 -> 4; matrix products, arithmetic and copies ran while one was open for 3% -> 25% of each run, Pallas kernels for 0% -> 0%
where the time goes in v1:
time: 136 us; the launch traced here: 135 us
  waiting for transfers between devices  47 us (35%)
  local copies, waits for them, and re-layouts  29.4 us (22%)
  matrix products  22.5 us (17%)
  starting transfers between devices  18.3 us (13%)
  other arithmetic  17.1 us (13%)
    all_to_all x1, waiting for transfers between devices, local(): lax.all_to_all(fourier, ('ma', 'row'), split_axis=0, concat_axis=0, tiled...  25.9 us
    all_to_all x1, waiting for transfers between devices, local(): lax.all_to_all(to_rows, ('ma', 'row'), split_axis=0, concat_axis=0, tiled...  14.9 us
    cos x1, other arithmetic, fourier_table(): jnp.cos(angles)  13.6 us
    convert_element_type x3, local copies, waits for them, and re-layouts, fourier_table(): jnp.concatenate([jnp.cos(angles), -jnp.sin(angles)], axis=1).astype(BF16)  8.69 us
    dot_general x1, matrix products, local(): jnp.einsum('zlfhnr,znq->lfhrq', at_rows, table, preferred_element_type=F32)  6.91 us
    unnamed x6, local copies, waits for them, and re-layouts  5.89 us
    all_to_all x1, starting transfers between devices, local(): lax.all_to_all(to_rows, ('ma', 'row'), split_axis=0, concat_axis=0, tiled...  5.78 us
    all_to_all x1, waiting for transfers between devices, local(): lax.all_to_all(mixed, 'row', split_axis=0, concat_axis=0, tiled=True)  5.32 us
  transfers between devices with their start and end apart: 4, of which 4 were waited for; matrix products, arithmetic and copies ran while one was open for 25% of the time, Pallas kernels for 0%

profile of v1, /device:TPU:0, one launch (start us, length us, event | category | flops | bytes accessed | tf_op | source)
XLA Modules:
  0.0 135.3 jit_solution(3671188509814605274)
XLA Ops:
  0.6 2.3 %copy.100 = bf16[1,3,64,513,2]{3,4,1,0,2:T(2,128)(2,1)} copy(f32[1,3,64,513,2]{3,4,2,1,0:T(2,128)} %param.4) | data formatting | bytes 1181952 | tf_op args[0]
  2.9 5.2 %all-to-all-start = ((bf16[64,1,3,2,513]{4,3,2,1,0:T(2,128)(2,1)}), bf16[64,1,3,2,513]{4,3,2,1,0:T(2,128)(2,1)S(1)}, u32[]{:S(2)}, u32[]{:S(2)}) async-start(bf16[64,1,3,2,513]{4,3,2,1,0:T(2,128)(2,1)} %bitcast.92), calls=%async_computation | async-start | bytes 983040 | tf_op jit(solution)/shard_map/all_to_all | solution.py:85
  10.1 2.2 %constant_dynamic-slice_fusion = bf16[8,513,384]{2,0,1:T(8,128)(2,1)S(1)} fusion(bf16[64,513,384]{2,0,1:T(8,128)(2,1)} %param.5, s32[]{:T(128)S(6)} %select_n.89), kind=kLoop, calls=%fused_computation.97 | loop fusion | bytes 6303748 | tf_op jit(solution)/shard_map/dynamic_slice | solution.py:74
  12.3 4.4 %fusion.12 = bf16[8,513,512]{2,1,0:T(8,128)(2,1)} fusion(bf16[8,513,384]{2,0,1:T(8,128)(2,1)S(1)} %constant_dynamic-slice_fusion, s32[512]{0:T(512)S(1)} %pad_bitcast_fusion), kind=kOutput, calls=%fused_computation.18 | convolution fusion | flops 1616056320 | bytes 7356416 | tf_op jit(solution)/shard_map/sji,io->sjo/dot_general | solution.py:79
  18.5 1.7 %broadcast_multiply_fusion = bf16[8,8,3,2,2,2,513]{6,5,4,3,2,1,0:T(2,128)(2,1)S(1)} fusion(bf16[8,2,2,513]{3,2,1,0:T(2,128)(2,1)S(1)} %copy.56, bf16[8,8,3,2,513]{4,3,2,1,0:T(2,128)(2,1)S(1)} %copy.55), kind=kLoop, calls=%fused_computation.40 | loop fusion | flops 787968 | bytes 2002752 | tf_op jit(solution)/shard_map/mul | solution.py:93
  20.2 2.7 %mul.219 = bf16[8,192,513]{2,1,0:T(8,128)(2,1)} reshape(bf16[8,8,3,2,2,2,513]{6,5,4,3,2,1,0:T(2,128)(2,1)S(1)} %broadcast_multiply_fusion) | data formatting | bytes 3151872 | tf_op jit(solution)/shard_map/mul | solution.py:93
  22.9 4.2 %convolution_convert_fusion = bf16[8,192,512]{2,1,0:T(8,128)(2,1)S(1)} fusion(bf16[8,192,513]{2,1,0:T(8,128)(2,1)} %mul.219, bf16[8,513,512]{2,1,0:T(8,128)(2,1)} %fusion.12), kind=kOutput, calls=%fused_computation.21 | convolution fusion | flops 807665664 | bytes 7351296 | tf_op jit(solution)/shard_map/smj,sjo->smo/dot_general | solution.py:94
  27.5 2.1 %copy.58 = bf16[4,8,1,3,2,8,4,128]{7,6,5,4,3,1,0,2:T(4,128)(2,1)} copy(bf16[4,8,1,3,2,8,4,128]{7,0,6,4,3,1,5,2:T(4,128)(2,1)S(1)} %bitcast.95) | data formatting | bytes 3145728 | tf_op jit(solution)/shard_map/transpose | solution.py:98
  29.7 5.8 %all-to-all-start.1 = ((bf16[32,1,3,2,32,128]{5,4,3,2,1,0:T(8,128)(2,1)}), bf16[32,1,3,2,32,128]{5,4,3,2,1,0:T(8,128)(2,1)}, u32[]{:S(2)}, u32[]{:S(2)}) async-start(bf16[32,1,3,2,32,128]{5,4,3,2,1,0:T(8,128)(2,1)} %bitcast.13), calls=%async_computation.1 | async-start | bytes 3145728 | tf_op jit(solution)/shard_map/all_to_all | solution.py:100
  35.5 13.6 %fusion.10 = (bf16[256,1,2,1536]{3,0,2,1:T(8,128)(2,1)S(1)}, bf16[256,1,2,1536]{3,0,2,1:T(8,128)(2,1)S(1)}) fusion(s32[256,2]{0,1:T(2,128)S(1)} %pad_add_fusion), kind=kLoop, calls=%fused_computation.16 | loop fusion | flops 9437184 | bytes 3147776 | tf_op jit(solution)/shard_map/cos | solution.py:43
  49.4 3.2 %copy.60 = bf16[256,2,2,1536]{3,2,1,0:T(2,128)(2,1)S(1)} copy(bf16[256,2,2,1536]{3,0,2,1:T(8,128)(2,1)S(1)} %maximum_convert_fusion) | data formatting | bytes 6291456 | tf_op jit(solution)/shard_map/convert_element_type | solution.py:43
  52.7 2.7 %convert_element_type.155 = bf16[32,32,1536]{2,1,0:T(8,128)(2,1)} reshape(bf16[256,2,2,1536]{3,2,1,0:T(2,128)(2,1)S(1)} %copy.60) | data formatting | bytes 6291456 | tf_op jit(solution)/shard_map/convert_element_type | solution.py:43
  55.4 2.7 %reshape.610 = bf16[32,32,1536,1,1]{2,1,0,3,4:T(8,128)(2,1)} reshape(bf16[256,2,2,1536]{3,2,1,0:T(2,128)(2,1)S(1)} %copy.60) | data formatting | bytes 6291456 | tf_op jit(solution)/shard_map/convert_element_type | solution.py:43
  58.1 14.9 %all-to-all-done.1 = bf16[32,1,3,2,32,128]{5,4,3,2,1,0:T(8,128)(2,1)} async-done(((bf16[32,1,3,2,32,128]{5,4,3,2,1,0:T(8,128)(2,1)}), bf16[32,1,3,2,32,128]{5,4,3,2,1,0:T(8,128)(2,1)}, u32[]{:S(2)}, u32[]{:S(2)}) %all-to-all-start.1) | async-done | bytes 1572896 | tf_op jit(solution)/shard_map/all_to_all | solution.py:100
  73.0 6.9 %convolution_bitcast_fusion = f32[1,3,2,128,1536]{4,3,2,1,0:T(8,128)S(1)} fusion(bf16[32,32,1536,1,1]{2,1,0,4,3:T(8,128)(2,1)} %bitcast.94, bf16[32,1,3,2,32,128]{5,4,3,2,1,0:T(8,128)(2,1)} %all-to-all-done.1), kind=kOutput, calls=%fused_computation.2 | convolution fusion | flops 2415919104 | bytes 9437184 | tf_op jit(solution)/shard_map/zlfhnr,znq->lfhrq/dot_general | solution.py:102
  80.6 1.3 copy-done
  82.0 1.8 %fusion.22 = bf16[32,1,2,2,32,128]{5,4,0,3,2,1:T(8,128)(2,1)S(1)} fusion(bf16[32,32,1536,1,1]{2,1,0,3,4:T(8,128)(2,1)S(1)} %copy-done, bf16[1,2,2,128,1536]{4,3,2,1,0:T(8,128)(2,1)S(1)} %fusion.4), kind=kOutput, calls=%fused_computation.26 | convolution fusion | flops 1611661312 | bytes 5767168 | tf_op jit(solution)/shard_map/znq,lghrq->zlghnr/dot_general | solution.py:104
  83.8 1.1 copy.62
  84.9 3.7 %all-to-all-start.2 = ((bf16[32,1,2,2,32,128]{5,4,3,2,1,0:T(8,128)(2,1)}), bf16[32,1,2,2,32,128]{5,4,3,2,1,0:T(8,128)(2,1)S(1)}, u32[]{:S(2)}, u32[]{:S(2)}) async-start(bf16[32,1,2,2,32,128]{5,4,3,2,1,0:T(8,128)(2,1)} %copy.62), calls=%async_computation.2 | async-start | bytes 2097152 | tf_op jit(solution)/shard_map/all_to_all | solution.py:107
  89.0 25.9 %all-to-all-done.2 = bf16[32,1,2,2,32,128]{5,4,3,2,1,0:T(8,128)(2,1)S(1)} async-done(((bf16[32,1,2,2,32,128]{5,4,3,2,1,0:T(8,128)(2,1)}), bf16[32,1,2,2,32,128]{5,4,3,2,1,0:T(8,128)(2,1)S(1)}, u32[]{:S(2)}, u32[]{:S(2)}) %all-to-all-start.2) | async-done | bytes 1048608 | tf_op jit(solution)/shard_map/all_to_all | solution.py:107
  116.9 3.9 %fusion.28 = f32[8,128,513]{2,1,0:T(8,128)S(1)} fusion(bf16[8,513,512]{2,1,0:T(8,128)(2,1)} %fusion.12, bf16[8,128,128]{2,1,0:T(8,128)(2,1)S(1)} %bitcast.105, bf16[8,128,128]{2,1,0:T(8,128)(2,1)S(1)} %bitcast.106, bf16[8,128,128]{2,1,0:T(8,128)(2,1)S(1)} %bitcast.107, bf16[8,128,128]{2,1,0:T(8,128)(2,1)S(1)} %bitcast.104), kind=kOutput, calls=%fused_computation.30 | convolution fusion | flops 542113792 | bytes 7352320 | tf_op jit(solution)/shard_map/smo,sjo->smj/dot_general | solution.py:113
  122.8 3.7 %all-to-all-start.3 = ((bf16[8,1,2,8,2,513]{5,4,2,3,1,0:T(2,128)(2,1)}), bf16[8,1,2,8,2,513]{5,4,2,3,1,0:T(2,128)(2,1)S(1)}, u32[]{:S(2)}, u32[]{:S(2)}) async-start(bf16[8,1,2,8,2,513]{5,4,2,3,1,0:T(2,128)(2,1)} %bitcast.93), calls=%async_computation.3 | async-start | bytes 655360 | tf_op jit(solution)/shard_map/all_to_all | solution.py:121
  126.6 2.2 %copy.68 = bf16[1,192,2,1536]{3,2,1,0:T(2,128)(2,1)} copy(bf16[1,192,2,1536]{3,1,2,0:T(8,128)(2,1)S(1)} %bitcast.96) | data formatting | bytes 2359296
  128.8 5.3 %all-to-all-done.3 = bf16[8,1,2,8,2,513]{5,4,2,3,1,0:T(2,128)(2,1)S(1)} async-done(((bf16[8,1,2,8,2,513]{5,4,2,3,1,0:T(2,128)(2,1)}), bf16[8,1,2,8,2,513]{5,4,2,3,1,0:T(2,128)(2,1)S(1)}, u32[]{:S(2)}, u32[]{:S(2)}) %all-to-all-start.3) | async-done | bytes 262688 | tf_op jit(solution)/shard_map/all_to_all | solution.py:121
  (41 shorter events, 10.5 us)
Async XLA Ops:
  2.9 14.6 %all-to-all-start = ((bf16[64,1,3,2,513]{4,3,2,1,0:T(2,128)(2,1)}), bf16[64,1,3,2,513]{4,3,2,1,0:T(2,128)(2,1)S(1)}, u32[]{:S(2)}, u32[]{:S(2)}) async-start(bf16[64,1,3,2,513]{4,3,2,1,0:T(2,128)(2,1)} %bitcast.92), calls=%async_computation | async-start | bytes 983040 | tf_op jit(solution)/shard_map/all_to_all | solution.py:85
  27.5 7.9 %copy-start.1 = (s32[256]{0:T(256)S(1)}, s32[256]{0:T(256)}, u32[]{:S(2)}) copy-start(s32[256]{0:T(256)} %param.6) | copy-start | bytes 3076
  29.7 43.4 %all-to-all-start.1 = ((bf16[32,1,3,2,32,128]{5,4,3,2,1,0:T(8,128)(2,1)}), bf16[32,1,3,2,32,128]{5,4,3,2,1,0:T(8,128)(2,1)}, u32[]{:S(2)}, u32[]{:S(2)}) async-start(bf16[32,1,3,2,32,128]{5,4,3,2,1,0:T(8,128)(2,1)} %bitcast.13), calls=%async_computation.1 | async-start | bytes 3145728 | tf_op jit(solution)/shard_map/all_to_all | solution.py:100
  80.1 1.9 %copy-start = (bf16[32,32,1536,1,1]{2,1,0,3,4:T(8,128)(2,1)S(1)}, bf16[32,32,1536,1,1]{2,1,0,3,4:T(8,128)(2,1)}, u32[]{:S(2)}) copy-start(bf16[32,32,1536,1,1]{2,1,0,3,4:T(8,128)(2,1)} %reshape.610) | copy-start | bytes 9437188
  84.9 30.0 %all-to-all-start.2 = ((bf16[32,1,2,2,32,128]{5,4,3,2,1,0:T(8,128)(2,1)}), bf16[32,1,2,2,32,128]{5,4,3,2,1,0:T(8,128)(2,1)S(1)}, u32[]{:S(2)}, u32[]{:S(2)}) async-start(bf16[32,1,2,2,32,128]{5,4,3,2,1,0:T(8,128)(2,1)} %copy.62), calls=%async_computation.2 | async-start | bytes 2097152 | tf_op jit(solution)/shard_map/all_to_all | solution.py:107
  122.8 11.3 %all-to-all-start.3 = ((bf16[8,1,2,8,2,513]{5,4,2,3,1,0:T(2,128)(2,1)}), bf16[8,1,2,8,2,513]{5,4,2,3,1,0:T(2,128)(2,1)S(1)}, u32[]{:S(2)}, u32[]{:S(2)}) async-start(bf16[8,1,2,8,2,513]{5,4,2,3,1,0:T(2,128)(2,1)} %bitcast.93), calls=%async_computation.3 | async-start | bytes 655360 | tf_op jit(solution)/shard_map/all_to_all | solution.py:121

commit v2 on v1

--- a/solution.py
+++ b/solution.py
@@ -7,7 +7,6 @@
 NPHI = 1536
 NPAIRS = 256
 PACK = 513
-LANES = 128
 
 HIGH = lax.Precision.HIGHEST
 BF16 = jnp.bfloat16
@@ -49,7 +48,6 @@
     levels = lev * row
     half = legendre.shape[2]
     own = half // ma
-    width = -(-own // LANES) * LANES
     share = -(-slots // row)
     extra = share * row - slots
     devices = ma * row
@@ -72,10 +70,7 @@
         functions = jnp.take(legendre, chosen, axis=0)
     else:
         functions = lax.dynamic_slice_in_dim(legendre, place * share, share, 0)
-    owners = jnp.pad(
-        theta_owner.reshape(ma, own), ((0, 0), (0, width - own)), constant_values=-1
-    ).reshape(-1)
-    order_rows = (jnp.arange(half)[:, None] == owners[None, :]).astype(BF16)
+    order_rows = (jnp.arange(half)[:, None] == theta_owner[None, :]).astype(BF16)
     functions = jnp.einsum(
         "sji,io->sjo", functions, order_rows, preferred_element_type=F32
     ).astype(BF16)
@@ -88,28 +83,41 @@
         "kzl,zslfcj->ksfcj", synth_mat.reshape(levels, row, lev), incoming, precision=HIGH
     ).astype(BF16)
 
-    spread = jnp.transpose(level_coeffs, (1, 0, 2, 3, 4))[:, :, :, None, :, None, :]
-    sel = jnp.transpose(synth_weights, (0, 2, 1, 3)).astype(BF16)[:, None, None, :, None, :, :]
-    weighted = (spread * sel).reshape(share, levels * fields * 8, PACK)
+    spread = jnp.transpose(level_coeffs, (1, 2, 0, 3, 4))[:, :, None, :, :, None, :]
+    sel = jnp.transpose(synth_weights, (0, 2, 1, 3)).astype(BF16)[:, None, :, None, None, :, :]
+    weighted = (spread * sel).reshape(share, fields * 2 * levels * 4, PACK)
     north_south = jnp.einsum(
         "smj,sjo->smo", weighted, functions, preferred_element_type=F32
     ).astype(BF16)
-    north_south = north_south.reshape(share, row, lev, fields, 2, 4, ma, width)
-    to_rows = jnp.transpose(north_south, (6, 1, 2, 3, 4, 0, 5, 7))
-    to_rows = to_rows.reshape(devices, lev, fields, 2, share * 4, width)
+    north_south = north_south.reshape(share, fields * 2, row, lev, 4, half)
+    to_rows = [
+        jnp.concatenate(
+            [north_south[:, x, ..., d * own : (d + 1) * own] for x in range(fields * 2)], axis=-1
+        )
+        for d in range(ma)
+    ]
+    to_rows = jnp.transpose(jnp.stack(to_rows), (0, 2, 3, 1, 4, 5))
+    to_rows = to_rows.reshape(devices, lev, share * 4, fields * 2 * own)
     at_rows = lax.all_to_all(to_rows, ("ma", "row"), split_axis=0, concat_axis=0, tiled=True)
 
-    grid = jnp.einsum("zlfhnr,znq->lfhrq", at_rows, table, preferred_element_type=F32)
+    grid = jnp.einsum("zlnm,znq->lmq", at_rows, table, preferred_element_type=F32)
+    grid = grid.reshape(lev, fields, 2 * own, NPHI)
     flux = (grid[:, 0:1] * grid[:, 1:3]).astype(BF16)
-    fourier = jnp.einsum("znq,lghrq->zlghnr", table, flux, preferred_element_type=F32)
+    fourier = jnp.einsum(
+        "znq,lmq->zlnm", table, flux.reshape(lev, 4 * own, NPHI), preferred_element_type=F32
+    )
     fourier = (fourier * NPHI ** (-0.5)).astype(BF16)
-    flux_grid = jnp.transpose(flux[:, :, :, :own], (0, 2, 3, 1, 4)).reshape(lev, 2 * own, 2, NPHI)
+    flux_grid = jnp.transpose(flux, (0, 2, 1, 3))
     back = lax.all_to_all(fourier, ("ma", "row"), split_axis=0, concat_axis=0, tiled=True)
 
-    back = back.reshape(ma, row, lev, 2, 2, share, 2, 2, width)
-    back = jnp.transpose(back, (0, 5, 7, 4, 1, 2, 3, 6, 8))
-    back = back.reshape(ma, share, 4 * levels * 4, width)
-    values = jnp.concatenate([back[d] for d in range(ma)], axis=-1)
+    back = back.reshape(ma, row, lev, share, 2, 2, 4 * own)
+    values = [
+        jnp.concatenate([back[d, ..., x * own : (x + 1) * own] for d in range(ma)], axis=-1)
+        for x in range(4)
+    ]
+    values = jnp.stack(values).reshape(2, 2, row, lev, share, 2, 2, half)
+    values = jnp.transpose(values, (4, 6, 1, 2, 3, 0, 5, 7))
+    values = values.reshape(share, 4 * levels * 4, half)
     product = jnp.einsum("smo,sjo->smj", values, functions, preferred_element_type=F32)
     product = product.reshape(share, 4, levels * 4, PACK)
     spectral = jnp.sum(product * weights.reshape(share, 4, 1, PACK), axis=1)

time: 136 us -> 145 us (1.066)
  local copies, waits for them, and re-layouts: 29.4 us -> 48.2 us
  waiting for transfers between devices: 47 us -> 33.9 us
  other arithmetic: 17.1 us -> 23.1 us
  matrix products: 22.5 us -> 20.2 us
    all_to_all x1, waiting for transfers between devices: 25.9 us -> 17 us  [local(): lax.all_to_all(fourier, ('ma', 'row'), split_axis=0, concat_axis=0, tiled...]
    all_to_all x1, waiting for transfers between devices: 14.9 us -> 9.3 us  [local(): lax.all_to_all(to_rows, ('ma', 'row'), split_axis=0, concat_axis=0, tiled...]
    another operation x0 -> x2, local copies, waits for them, and re-layouts: none -> 5.55 us
    reshape x3, local copies, waits for them, and re-layouts: 2.21 us -> 6.9 us  [the longest x1 2.95 us: local(): values = values.reshape(share, 4 * levels * 4, half)]
    all_to_all x1, waiting for transfers between devices: 0.82 us -> 3.77 us  [local(): lax.all_to_all(outgoing, 'row', split_axis=0, concat_axis=0, tiled=True)]
    reshape x2, local copies, waits for them, and re-layouts: 1.09 us -> 3.75 us  [local(): mixed = mixed.reshape(row, lev, 2, 2, share, PACK)]
    mul x1, local copies, waits for them, and re-layouts: 2.73 us -> 5.22 us  [local(): weighted = (spread * sel).reshape(share, fields * 2 * levels * 4, PACK)]
    dot_general x1, matrix products: 4.42 us -> 2.43 us  [local(): jnp.einsum('sji,io->sjo', functions, order_rows, preferred_element_type=F32)]
where the time goes in v2:
time: 145 us; the launch traced here: 144 us
  local copies, waits for them, and re-layouts  48.2 us (33%)
  waiting for transfers between devices  33.9 us (23%)
  other arithmetic  23.1 us (16%)
  matrix products  20.2 us (14%)
  starting transfers between devices  17.7 us (12%)
    all_to_all x1, waiting for transfers between devices, local(): lax.all_to_all(fourier, ('ma', 'row'), split_axis=0, concat_axis=0, tiled...  17 us
    cos x1, other arithmetic, fourier_table(): jnp.cos(angles)  13.6 us
    all_to_all x1, waiting for transfers between devices, local(): lax.all_to_all(to_rows, ('ma', 'row'), split_axis=0, concat_axis=0, tiled...  9.3 us
    convert_element_type x3, local copies, waits for them, and re-layouts, fourier_table(): jnp.concatenate([jnp.cos(angles), -jnp.sin(angles)], axis=1).astype(BF16)  8.68 us
    unnamed x38, local copies, waits for them, and re-layouts  6.79 us
    another operation x1, local copies, waits for them, and re-layouts  5.28 us
    mul x1, local copies, waits for them, and re-layouts, local(): weighted = (spread * sel).reshape(share, fields * 2 * levels * 4, PACK)  5.22 us
    all_to_all x1, starting transfers between devices, local(): lax.all_to_all(outgoing, 'row', split_axis=0, concat_axis=0, tiled=True)  5.17 us
  transfers between devices with their start and end apart: 4, of which 4 were waited for; matrix products, arithmetic and copies ran while one was open for 25% of the time, Pallas kernels for 0%

profile of v2, /device:TPU:0, one launch (start us, length us, event | category | flops | bytes accessed | tf_op | source)
XLA Modules:
  0.0 144.3 jit_solution(5400283152712093510)
XLA Ops:
  0.6 2.3 %copy.405 = bf16[1,3,64,513,2]{3,4,1,0,2:T(2,128)(2,1)} copy(f32[1,3,64,513,2]{3,4,2,1,0:T(2,128)} %param.4) | data formatting | bytes 1181952 | tf_op args[0]
  3.0 5.2 %all-to-all-start = ((bf16[64,1,3,2,513]{4,3,2,1,0:T(2,128)(2,1)}), bf16[64,1,3,2,513]{4,3,2,1,0:T(2,128)(2,1)}, u32[]{:S(2)}, u32[]{:S(2)}) async-start(bf16[64,1,3,2,513]{4,3,2,1,0:T(2,128)(2,1)} %bitcast.203), calls=%async_computation | async-start | bytes 983040 | tf_op jit(solution)/shard_map/all_to_all | solution.py:80
  11.4 2.4 %fusion.9 = bf16[8,513,384]{2,1,0:T(8,128)(2,1)S(1)} fusion(bf16[8,513,384]{2,0,1:T(8,128)(2,1)S(1)} %constant_dynamic-slice_fusion, s32[384]{0:T(512)S(1)} %copy-done.5), kind=kOutput, calls=%fused_computation.16 | convolution fusion | flops 1212042240 | bytes 6305280 | tf_op jit(solution)/shard_map/sji,io->sjo/dot_general | solution.py:74
  13.9 3.8 %all-to-all-done = bf16[64,1,3,2,513]{4,3,2,1,0:T(2,128)(2,1)} async-done(((bf16[64,1,3,2,513]{4,3,2,1,0:T(2,128)(2,1)}), bf16[64,1,3,2,513]{4,3,2,1,0:T(2,128)(2,1)}, u32[]{:S(2)}, u32[]{:S(2)}) %all-to-all-start) | async-done | bytes 394016 | tf_op jit(solution)/shard_map/all_to_all | solution.py:80
  19.6 3.0 %broadcast_multiply_fusion = bf16[8,3,2,8,2,2,513]{6,5,4,3,2,1,0:T(2,128)(2,1)} fusion(bf16[8,2,2,513]{3,2,1,0:T(2,128)(2,1)S(1)} %copy.266, bf16[8,3,8,2,513]{4,3,2,1,0:T(2,128)(2,1)S(1)} %copy.265), kind=kLoop, calls=%fused_computation.27 | loop fusion | flops 787968 | bytes 2002752 | tf_op jit(solution)/shard_map/mul | solution.py:88
  22.6 5.2 %mul.219 = bf16[8,192,513]{2,1,0:T(8,128)(2,1)} reshape(bf16[8,3,2,8,2,2,513]{6,5,4,3,2,1,0:T(2,128)(2,1)} %broadcast_multiply_fusion) | data formatting | bytes 3151872 | tf_op jit(solution)/shard_map/mul | solution.py:88
  27.9 3.9 %convolution_convert_fusion = bf16[8,192,384]{2,1,0:T(8,128)(2,1)} fusion(bf16[8,192,513]{2,1,0:T(8,128)(2,1)} %mul.219, bf16[8,513,384]{2,1,0:T(8,128)(2,1)S(1)} %fusion.9), kind=kOutput, calls=%fused_computation.19 | convolution fusion | flops 605749248 | bytes 5907456 | tf_op jit(solution)/shard_map/smj,sjo->smo/dot_general | solution.py:89
  31.7 2.5 %reshape.596 = bf16[8,6,8,1,4,384]{5,4,2,1,0,3:T(4,128)(2,1)S(1)} reshape(bf16[8,192,384]{2,1,0:T(8,128)(2,1)} %convolution_convert_fusion) | data formatting | bytes 2359296 | tf_op jit(solution)/shard_map/reshape | solution.py:92
  38.2 4.6 %all-to-all-start.1 = ((bf16[32,1,32,576]{3,2,1,0:T(8,128)(2,1)}), bf16[32,1,32,576]{3,2,1,0:T(8,128)(2,1)}, u32[]{:S(2)}, u32[]{:S(2)}) async-start(bf16[32,1,32,576]{3,2,1,0:T(8,128)(2,1)} %copy.292), calls=%async_computation.1 | async-start | bytes 2621440 | tf_op jit(solution)/shard_map/all_to_all | solution.py:101
  42.9 13.6 %fusion.6 = (bf16[256,1,2,1536]{3,0,2,1:T(8,128)(2,1)S(1)}, bf16[256,1,2,1536]{3,0,2,1:T(8,128)(2,1)S(1)}) fusion(s32[256,2]{0,1:T(2,128)S(1)} %pad_add_fusion), kind=kLoop, calls=%fused_computation.11 | loop fusion | flops 9437184 | bytes 3147776 | tf_op jit(solution)/shard_map/cos | solution.py:42
  56.8 3.2 %copy.294 = bf16[256,2,2,1536]{3,2,1,0:T(2,128)(2,1)S(1)} copy(bf16[256,2,2,1536]{3,0,2,1:T(8,128)(2,1)S(1)} %maximum_convert_fusion) | data formatting | bytes 6291456 | tf_op jit(solution)/shard_map/convert_element_type | solution.py:42
  60.0 2.8 %reshape.609 = bf16[32,32,1536,1]{2,1,0,3:T(8,128)(2,1)} reshape(bf16[256,2,2,1536]{3,2,1,0:T(2,128)(2,1)S(1)} %copy.294) | data formatting | bytes 6291456 | tf_op jit(solution)/shard_map/convert_element_type | solution.py:42
  62.8 2.7 %convert_element_type.155 = bf16[32,32,1536]{2,1,0:T(8,128)(2,1)} reshape(bf16[256,2,2,1536]{3,2,1,0:T(2,128)(2,1)S(1)} %copy.294) | data formatting | bytes 6291456 | tf_op jit(solution)/shard_map/convert_element_type | solution.py:42
  65.5 9.3 %all-to-all-done.1 = bf16[32,1,32,576]{3,2,1,0:T(8,128)(2,1)} async-done(((bf16[32,1,32,576]{3,2,1,0:T(8,128)(2,1)}), bf16[32,1,32,576]{3,2,1,0:T(8,128)(2,1)}, u32[]{:S(2)}, u32[]{:S(2)}) %all-to-all-start.1) | async-done | bytes 1179680 | tf_op jit(solution)/shard_map/all_to_all | solution.py:101
  74.8 5.3 %reshape.613 = bf16[3,192,32,32]{1,0,2,3:T(4,128)(2,1)} reshape(bf16[576,32,32]{0,1,2:T(8,128)(2,1)} %bitcast.42) | data formatting | bytes 2359296 | tf_op jit(solution)/shard_map/reshape.180
  80.0 4.6 %convolution_bitcast_fusion = f32[1,3,192,1536]{3,2,1,0:T(8,128)S(1)} fusion(bf16[32,32,1536,1]{2,1,0,3:T(8,128)(2,1)} %reshape.609, bf16[3,192,32,32]{1,0,2,3:T(4,128)(2,1)} %reshape.613), kind=kOutput, calls=%fused_computation.2 | convolution fusion | flops 1811939328 | bytes 7864320 | tf_op jit(solution)/shard_map/zlnm,znq->lmq/dot_general | solution.py:103
  87.0 2.7 %fusion.13 = bf16[32,1,32,384]{3,2,1,0:T(8,128)(2,1)} fusion(bf16[384,1536,1]{1,0,2:T(8,128)(2,1)S(1)} %bitcast.239, bf16[32,32,1536]{2,1,0:T(8,128)(2,1)S(1)} %copy-done.2), kind=kOutput, calls=%fused_computation.21 | convolution fusion | flops 1208745984 | bytes 5111808 | tf_op jit(solution)/shard_map/znq,lmq->zlnm/dot_general | solution.py:106
  89.7 3.9 %all-to-all-start.2 = ((bf16[32,1,32,384]{3,2,1,0:T(8,128)(2,1)}), bf16[32,1,32,384]{3,2,1,0:T(8,128)(2,1)}, u32[]{:S(2)}, u32[]{:S(2)}) async-start(bf16[32,1,32,384]{3,2,1,0:T(8,128)(2,1)} %fusion.13), calls=%async_computation.2 | async-start | bytes 1572864 | tf_op jit(solution)/shard_map/all_to_all | solution.py:111
  97.0 17.0 %all-to-all-done.2 = bf16[32,1,32,384]{3,2,1,0:T(8,128)(2,1)} async-done(((bf16[32,1,32,384]{3,2,1,0:T(8,128)(2,1)}), bf16[32,1,32,384]{3,2,1,0:T(8,128)(2,1)}, u32[]{:S(2)}, u32[]{:S(2)}) %all-to-all-start.2) | async-done | bytes 786464 | tf_op jit(solution)/shard_map/all_to_all | solution.py:111
  118.4 2.9 %reshape.603 = bf16[8,128,384]{2,1,0:T(8,128)(2,1)} reshape(bf16[8,2,2,8,1,2,2,384]{7,6,5,3,2,1,0,4:T(2,128)(2,1)} %copy.314) | data formatting | bytes 1572864 | tf_op jit(solution)/shard_map/reshape | solution.py:120
  121.3 3.6 %fusion.58 = f32[8,128,513]{2,1,0:T(8,128)S(1)} fusion(bf16[8,128,384]{2,1,0:T(8,128)(2,1)} %reshape.603, bf16[8,513,384]{2,1,0:T(8,128)(2,1)} %copy-done), kind=kOutput, calls=%fused_computation.141 | convolution fusion | flops 403439616 | bytes 6039552 | tf_op jit(solution)/shard_map/smo,sjo->smj/dot_general | solution.py:121
  130.4 4.1 %all-to-all-start.3 = ((bf16[8,1,2,8,2,513]{5,4,2,3,1,0:T(2,128)(2,1)}), bf16[8,1,2,8,2,513]{5,4,2,3,1,0:T(2,128)(2,1)}, u32[]{:S(2)}, u32[]{:S(2)}) async-start(bf16[8,1,2,8,2,513]{5,4,2,3,1,0:T(2,128)(2,1)} %bitcast.238), calls=%async_computation.3 | async-start | bytes 655360 | tf_op jit(solution)/shard_map/all_to_all | solution.py:129
  136.1 2.2 %copy.319 = bf16[1,192,2,1536]{3,2,1,0:T(2,128)(2,1)} copy(bf16[1,192,2,1536]{3,1,2,0:T(8,128)(2,1)S(1)} %fusion.68) | data formatting | bytes 2359296
  138.3 3.8 %all-to-all-done.3 = bf16[8,1,2,8,2,513]{5,4,2,3,1,0:T(2,128)(2,1)} async-done(((bf16[8,1,2,8,2,513]{5,4,2,3,1,0:T(2,128)(2,1)}), bf16[8,1,2,8,2,513]{5,4,2,3,1,0:T(2,128)(2,1)}, u32[]{:S(2)}, u32[]{:S(2)}) %all-to-all-start.3) | async-done | bytes 262688 | tf_op jit(solution)/shard_map/all_to_all | solution.py:129
  (86 shorter events, 28.5 us)
Async XLA Ops:
  0.6 7.5 %copy-start.4 = (s32[256]{0:T(256)S(1)}, s32[256]{0:T(256)}, u32[]{:S(2)}) copy-start(s32[256]{0:T(256)} %param.6) | copy-start | bytes 3076
  3.0 14.7 %all-to-all-start = ((bf16[64,1,3,2,513]{4,3,2,1,0:T(2,128)(2,1)}), bf16[64,1,3,2,513]{4,3,2,1,0:T(2,128)(2,1)}, u32[]{:S(2)}, u32[]{:S(2)}) async-start(bf16[64,1,3,2,513]{4,3,2,1,0:T(2,128)(2,1)} %bitcast.203), calls=%async_computation | async-start | bytes 983040 | tf_op jit(solution)/shard_map/all_to_all | solution.py:80
  9.2 2.2 %copy-start.5 = (s32[384]{0:T(512)S(1)}, s32[384]{0:T(512)}, u32[]{:S(2)}) copy-start(s32[384]{0:T(512)} %param.7) | copy-start | bytes 4612
  13.8 14.0 %copy-start = (bf16[8,513,384]{2,1,0:T(8,128)(2,1)}, bf16[8,513,384]{2,1,0:T(8,128)(2,1)S(1)}, u32[]{:S(2)}) copy-start(bf16[8,513,384]{2,1,0:T(8,128)(2,1)S(1)} %fusion.9) | copy-start | bytes 9455620
  38.2 36.5 %all-to-all-start.1 = ((bf16[32,1,32,576]{3,2,1,0:T(8,128)(2,1)}), bf16[32,1,32,576]{3,2,1,0:T(8,128)(2,1)}, u32[]{:S(2)}, u32[]{:S(2)}) async-start(bf16[32,1,32,576]{3,2,1,0:T(8,128)(2,1)} %copy.292), calls=%async_computation.1 | async-start | bytes 2621440 | tf_op jit(solution)/shard_map/all_to_all | solution.py:101
  84.7 1.0 copy-start.1
  84.7 2.3 %copy-start.2 = (bf16[32,32,1536]{2,1,0:T(8,128)(2,1)S(1)}, bf16[32,32,1536]{2,1,0:T(8,128)(2,1)}, u32[]{:S(2)}) copy-start(bf16[32,32,1536]{2,1,0:T(8,128)(2,1)} %convert_element_type.155) | copy-start | bytes 9437188
  89.7 24.3 %all-to-all-start.2 = ((bf16[32,1,32,384]{3,2,1,0:T(8,128)(2,1)}), bf16[32,1,32,384]{3,2,1,0:T(8,128)(2,1)}, u32[]{:S(2)}, u32[]{:S(2)}) async-start(bf16[32,1,32,384]{3,2,1,0:T(8,128)(2,1)} %fusion.13), calls=%async_computation.2 | async-start | bytes 1572864 | tf_op jit(solution)/shard_map/all_to_all | solution.py:111
  121.3 3.6 %copy-start.3 = (f32[8,4,513]{2,1,0:T(4,128)S(1)}, f32[8,4,513]{2,1,0:T(4,128)}, u32[]{:S(2)}) copy-start(f32[8,4,513]{2,1,0:T(4,128)} %copy.316) | copy-start | bytes 196996
  130.4 11.7 %all-to-all-start.3 = ((bf16[8,1,2,8,2,513]{5,4,2,3,1,0:T(2,128)(2,1)}), bf16[8,1,2,8,2,513]{5,4,2,3,1,0:T(2,128)(2,1)}, u32[]{:S(2)}, u32[]{:S(2)}) async-start(bf16[8,1,2,8,2,513]{5,4,2,3,1,0:T(2,128)(2,1)} %bitcast.238), calls=%async_computation.3 | async-start | bytes 655360 | tf_op jit(solution)/shard_map/all_to_all | solution.py:129

commit v3 on v1

--- a/solution.py
+++ b/solution.py
@@ -99,25 +99,38 @@
     to_rows = to_rows.reshape(devices, lev, fields, 2, share * 4, width)
     at_rows = lax.all_to_all(to_rows, ("ma", "row"), split_axis=0, concat_axis=0, tiled=True)
 
-    grid = jnp.einsum("zlfhnr,znq->lfhrq", at_rows, table, preferred_element_type=F32)
-    flux = (grid[:, 0:1] * grid[:, 1:3]).astype(BF16)
-    fourier = jnp.einsum("znq,lghrq->zlghnr", table, flux, preferred_element_type=F32)
-    fourier = (fourier * NPHI ** (-0.5)).astype(BF16)
-    flux_grid = jnp.transpose(flux[:, :, :, :own], (0, 2, 3, 1, 4)).reshape(lev, 2 * own, 2, NPHI)
-    back = lax.all_to_all(fourier, ("ma", "row"), split_axis=0, concat_axis=0, tiled=True)
+    def on_grid(values):
+        return jnp.einsum("zlfhnr,znq->lfhrq", values, table, preferred_element_type=F32)
 
-    back = back.reshape(ma, row, lev, 2, 2, share, 2, 2, width)
-    back = jnp.transpose(back, (0, 5, 7, 4, 1, 2, 3, 6, 8))
-    back = back.reshape(ma, share, 4 * levels * 4, width)
-    values = jnp.concatenate([back[d] for d in range(ma)], axis=-1)
-    product = jnp.einsum("smo,sjo->smj", values, functions, preferred_element_type=F32)
-    product = product.reshape(share, 4, levels * 4, PACK)
-    spectral = jnp.sum(product * weights.reshape(share, 4, 1, PACK), axis=1)
+    first = on_grid(at_rows[:, :, 0:2])
+    velocity = first[:, 0]
+    scalars = (first[:, 1], on_grid(at_rows[:, :, 2:3])[:, 0])
+    fluxes, parts = [], []
+    for scalar in scalars:
+        flux = (velocity * scalar).astype(BF16)
+        fluxes.append(flux)
+        fourier = jnp.einsum("znq,lhrq->zlhnr", table, flux, preferred_element_type=F32)
+        fourier = (fourier * NPHI ** (-0.5)).astype(BF16)
+        back = lax.all_to_all(fourier, ("ma", "row"), split_axis=0, concat_axis=0, tiled=True)
 
-    mix = jnp.kron(analysis_mat, jnp.eye(4, dtype=F32))
-    mixed = jnp.einsum("nk,skj->nsj", mix, spectral, precision=HIGH).astype(BF16)
-    mixed = mixed.reshape(row, lev, 2, 2, share, PACK)
-    mixed = jnp.transpose(mixed, (0, 1, 2, 4, 3, 5))
+        back = back.reshape(ma, row, lev, 2, share, 2, 2, width)
+        back = jnp.transpose(back, (0, 4, 6, 3, 1, 2, 5, 7))
+        back = back.reshape(ma, share, 4 * levels * 2, width)
+        values = jnp.concatenate([back[d] for d in range(ma)], axis=-1)
+        product = jnp.einsum("smo,sjo->smj", values, functions, preferred_element_type=F32)
+        product = product.reshape(share, 4, levels * 2, PACK)
+        parts.append(jnp.sum(product * weights.reshape(share, 4, 1, PACK), axis=1))
+    flux_grid = jnp.stack([flux[:, :, :own] for flux in fluxes], axis=3)
+    flux_grid = flux_grid.reshape(lev, 2 * own, 2, NPHI)
+
+    mix = jnp.kron(analysis_mat, jnp.eye(2, dtype=F32))
+    mixed = [
+        jnp.einsum("nk,skj->nsj", mix, part, precision=HIGH)
+        .astype(BF16)
+        .reshape(row, lev, 2, share, PACK)
+        for part in parts
+    ]
+    mixed = jnp.transpose(jnp.stack(mixed, axis=2), (0, 1, 2, 4, 3, 5))
     result = lax.all_to_all(mixed, "row", split_axis=0, concat_axis=0, tiled=True)
     result = jnp.transpose(result, (1, 2, 0, 3, 4, 5)).reshape(lev, 2, row * share, 2, PACK)
     flux_spectra = jnp.transpose(result[:, :, :slots], (0, 1, 2, 4, 3)).astype(F32)

time: 136 us -> 145 us (1.066)
  waiting for transfers between devices: 47 us -> 35 us
  local copies, waits for them, and re-layouts: 29.4 us -> 38.4 us
  other arithmetic: 17.1 us -> 21.5 us
  starting transfers between devices: 18.3 us -> 22.3 us
  matrix products: 22.5 us -> 26.3 us
    all_to_all x1, waiting for transfers between devices: 14.9 us -> 9.37 us  [local(): lax.all_to_all(to_rows, ('ma', 'row'), split_axis=0, concat_axis=0, tiled...]
    all_to_all x1 -> x2, waiting for transfers between devices: 25.9 us -> 21.3 us  [local(): lax.all_to_all(fourier, ('ma', 'row'), split_axis=0, concat_axis=0, tiled...]
    convert_element_type x3, local copies, waits for them, and re-layouts: 8.69 us -> 12.6 us  [fourier_table(): jnp.concatenate([jnp.cos(angles), -jnp.sin(angles)], axis=1).astype(BF16)]
    all_to_all x1 -> x2, starting transfers between devices: 3.73 us -> 7.48 us  [local(): lax.all_to_all(fourier, ('ma', 'row'), split_axis=0, concat_axis=0, tiled...]
    another operation x0 -> x2, other arithmetic: none -> 3.73 us  [the longest x1 3.69 us: local(): flux_grid = jnp.stack([flux[:, :, :own] for flux in fluxes], axis=3)]
    slice x1 -> x4, local copies, waits for them, and re-layouts: 0.08 us -> 2.9 us  [the longest x1 1.49 us: local(): scalars = (first[:, 1], on_grid(at_rows[:, :, 2:3])[:, 0])]
    dot_general x3 -> x6, matrix products: 9.41 us -> 11.9 us  [the longest x2 6.06 us: on_grid(): jnp.einsum('zlfhnr,znq->lfhrq', values, table, preferred_element_type=F32)]
    another operation x0 -> x7, local copies, waits for them, and re-layouts: none -> 2.09 us  [the longest x2 1.82 us: local(): flux_grid = jnp.stack([flux[:, :, :own] for flux in fluxes], axis=3)]
  transfers between devices with their start and end apart: 4 -> 5, of which waited for: 4 -> 5; matrix products, arithmetic and copies ran while one was open for 25% -> 33% of each run, Pallas kernels for 0% -> 0%
where the time goes in v3:
time: 145 us
  local copies, waits for them, and re-layouts  38.4 us (26%)
  waiting for transfers between devices  35 us (24%)
  matrix products  26.3 us (18%)
  starting transfers between devices  22.3 us (15%)
  other arithmetic  21.5 us (15%)
    all_to_all x2, waiting for transfers between devices, local(): lax.all_to_all(fourier, ('ma', 'row'), split_axis=0, concat_axis=0, tiled...  21.3 us
    cos x1, other arithmetic, fourier_table(): jnp.cos(angles)  13.6 us
    convert_element_type x3, local copies, waits for them, and re-layouts, fourier_table(): jnp.concatenate([jnp.cos(angles), -jnp.sin(angles)], axis=1).astype(BF16)  12.6 us
    all_to_all x1, waiting for transfers between devices, local(): lax.all_to_all(to_rows, ('ma', 'row'), split_axis=0, concat_axis=0, tiled...  9.37 us
    all_to_all x2, starting transfers between devices, local(): lax.all_to_all(fourier, ('ma', 'row'), split_axis=0, concat_axis=0, tiled...  7.48 us
    all_to_all x1, starting transfers between devices, local(): lax.all_to_all(to_rows, ('ma', 'row'), split_axis=0, concat_axis=0, tiled...  6.21 us
    dot_general x2, matrix products, on_grid(): jnp.einsum('zlfhnr,znq->lfhrq', values, table, preferred_element_type=F32)  6.06 us
    unnamed x20, local copies, waits for them, and re-layouts  5.36 us
  transfers between devices with their start and end apart: 5, of which 5 were waited for; matrix products, arithmetic and copies ran while one was open for 33% of the time, Pallas kernels for 0%

profile of v3, /device:TPU:0, one launch (start us, length us, event | category | flops | bytes accessed | tf_op | source)
XLA Modules:
  0.0 144.6 jit_solution(12681812884977898442)
XLA Ops:
  0.6 2.3 %copy.162 = bf16[1,3,64,513,2]{3,4,1,0,2:T(2,128)(2,1)} copy(f32[1,3,64,513,2]{3,4,2,1,0:T(2,128)} %param.4) | data formatting | bytes 1181952 | tf_op args[0]
  2.9 5.2 %all-to-all-start = ((bf16[64,1,3,2,513]{4,3,2,1,0:T(2,128)(2,1)}), bf16[64,1,3,2,513]{4,3,2,1,0:T(2,128)(2,1)S(1)}, u32[]{:S(2)}, u32[]{:S(2)}) async-start(bf16[64,1,3,2,513]{4,3,2,1,0:T(2,128)(2,1)} %bitcast.125), calls=%async_computation | async-start | bytes 983040 | tf_op jit(solution)/shard_map/all_to_all | solution.py:85
  10.3 2.2 %constant_dynamic-slice_fusion = bf16[8,513,384]{2,0,1:T(8,128)(2,1)S(1)} fusion(bf16[64,513,384]{2,0,1:T(8,128)(2,1)} %param.5, s32[]{:T(128)S(6)} %select_n.93), kind=kLoop, calls=%fused_computation.115 | loop fusion | bytes 6303748 | tf_op jit(solution)/shard_map/dynamic_slice | solution.py:74
  12.7 4.4 %fusion.18 = bf16[8,513,512]{2,1,0:T(8,128)(2,1)} fusion(bf16[8,513,384]{2,0,1:T(8,128)(2,1)S(1)} %constant_dynamic-slice_fusion, s32[512]{0:T(512)S(1)} %pad_bitcast_fusion), kind=kOutput, calls=%fused_computation.19 | convolution fusion | flops 1616056320 | bytes 7356416 | tf_op jit(solution)/shard_map/sji,io->sjo/dot_general | solution.py:79
  20.2 2.7 %mul.259 = bf16[8,192,513]{2,1,0:T(8,128)(2,1)} reshape(bf16[8,8,3,2,2,2,513]{6,5,4,3,2,1,0:T(2,128)(2,1)S(1)} %broadcast_multiply_fusion) | data formatting | bytes 3151872 | tf_op jit(solution)/shard_map/mul | solution.py:93
  22.9 4.2 %convolution_convert_fusion = bf16[8,192,512]{2,1,0:T(8,128)(2,1)S(1)} fusion(bf16[8,192,513]{2,1,0:T(8,128)(2,1)} %mul.259, bf16[8,513,512]{2,1,0:T(8,128)(2,1)} %fusion.18), kind=kOutput, calls=%fused_computation.21 | convolution fusion | flops 807665664 | bytes 7351296 | tf_op jit(solution)/shard_map/smj,sjo->smo/dot_general | solution.py:94
  27.5 2.1 %copy.100 = bf16[4,8,1,3,2,8,4,128]{7,6,5,4,3,1,0,2:T(4,128)(2,1)} copy(bf16[4,8,1,3,2,8,4,128]{7,0,6,4,3,1,5,2:T(4,128)(2,1)S(1)} %bitcast.129) | data formatting | bytes 3145728 | tf_op jit(solution)/shard_map/transpose | solution.py:98
  29.6 6.2 %all-to-all-start.1 = ((bf16[32,1,3,2,32,128]{5,4,3,2,1,0:T(8,128)(2,1)}), bf16[32,1,3,2,32,128]{5,4,3,2,1,0:T(8,128)(2,1)}, u32[]{:S(2)}, u32[]{:S(2)}) async-start(bf16[32,1,3,2,32,128]{5,4,3,2,1,0:T(8,128)(2,1)} %bitcast.12), calls=%async_computation.1 | async-start | bytes 3145728 | tf_op jit(solution)/shard_map/all_to_all | solution.py:100
  35.9 13.6 %fusion.10 = (bf16[256,1,2,1536]{3,0,2,1:T(8,128)(2,1)S(1)}, bf16[256,1,2,1536]{3,0,2,1:T(8,128)(2,1)S(1)}) fusion(s32[256,2]{0,1:T(2,128)S(1)} %pad_add_fusion), kind=kLoop, calls=%fused_computation.15 | loop fusion | flops 9437184 | bytes 3147776 | tf_op jit(solution)/shard_map/cos | solution.py:43
  49.8 3.2 %copy.102 = bf16[256,2,2,1536]{3,2,1,0:T(2,128)(2,1)S(1)} copy(bf16[256,2,2,1536]{3,0,2,1:T(8,128)(2,1)S(1)} %maximum_convert_fusion) | data formatting | bytes 6291456 | tf_op jit(solution)/shard_map/convert_element_type | solution.py:43
  54.7 2.8 %reshape.667 = bf16[32,32,1536,1]{2,1,0,3:T(8,128)(2,1)} reshape(bf16[256,2,2,1536]{3,2,1,0:T(2,128)(2,1)S(1)} %copy.102) | data formatting | bytes 6291456 | tf_op jit(solution)/shard_map/convert_element_type | solution.py:43
  57.5 6.5 %convert_element_type.193 = bf16[32,32,1536]{2,1,0:T(8,128)(2,1)S(1)} reshape(bf16[256,2,2,1536]{3,2,1,0:T(2,128)(2,1)} %copy-done) | data formatting | bytes 6291456 | tf_op jit(solution)/shard_map/convert_element_type | solution.py:43
  64.1 9.4 %all-to-all-done.1 = bf16[32,1,3,2,32,128]{5,4,3,2,1,0:T(8,128)(2,1)} async-done(((bf16[32,1,3,2,32,128]{5,4,3,2,1,0:T(8,128)(2,1)}), bf16[32,1,3,2,32,128]{5,4,3,2,1,0:T(8,128)(2,1)}, u32[]{:S(2)}, u32[]{:S(2)}) %all-to-all-start.1) | async-done | bytes 1572896 | tf_op jit(solution)/shard_map/all_to_all | solution.py:100
  74.8 3.4 %convolution_bitcast_fusion = f32[1,2,2,128,1536]{4,3,2,1,0:T(8,128)S(1)} fusion(bf16[32,32,1536,1,1]{2,1,0,4,3:T(8,128)(2,1)S(1)} %bitcast.128, bf16[32,1,2,2,32,128]{5,4,3,2,1,0:T(8,128)(2,1)S(1)} %slice.64), kind=kOutput, calls=%fused_computation.2 | convolution fusion | flops 1610612736 | bytes 7340032 | tf_op jit(solution)/shard_map/zlfhnr,znq->lfhrq/dot_general | solution.py:103
  79.7 2.6 %fusion.21 = bf16[2,128,1536]{2,1,0:T(8,128)(2,1)S(1)} fusion(bf16[32,32,1536]{2,1,0:T(8,128)(2,1)S(1)} %convert_element_type.193, f32[1,2,2,128,1536]{4,3,2,1,0:T(8,128)S(1)} %convolution_bitcast_fusion, bf16[32,1,1,2,32,128]{5,4,3,2,1,0:T(8,128)(2,1)S(1)} %slice.68), kind=kOutput, calls=%fused_computation.20 | convolution fusion | flops 806092800 | bytes 6029312 | tf_op jit(solution)/shard_map/zlfhnr,znq->lfhrq/dot_general | solution.py:103
  84.3 3.9 %all-to-all-start.3 = ((bf16[32,1,2,32,128]{4,3,2,1,0:T(8,128)(2,1)}), bf16[32,1,2,32,128]{4,3,2,1,0:T(8,128)(2,1)}, u32[]{:S(2)}, u32[]{:S(2)}) async-start(bf16[32,1,2,32,128]{4,3,2,1,0:T(8,128)(2,1)} %copy.111), calls=%async_computation.3 | async-start | bytes 1048576 | tf_op jit(solution)/shard_map/all_to_all | solution.py:114
  88.3 4.0 %fusion.27 = bf16[32,1,2,32,128]{4,3,0,2,1:T(8,128)(2,1)S(1)} fusion(bf16[32,32,1536,1]{2,1,0,3:T(8,128)(2,1)} %reshape.667, f32[1,2,2,128,1536]{4,3,2,1,0:T(8,128)} %copy-done.1), kind=kOutput, calls=%fused_computation.31 | convolution fusion | flops 806617088 | bytes 6815744 | tf_op jit(solution)/shard_map/znq,lhrq->zlhnr/dot_general | solution.py:112
  93.1 10.6 %all-to-all-done.3 = bf16[32,1,2,32,128]{4,3,2,1,0:T(8,128)(2,1)} async-done(((bf16[32,1,2,32,128]{4,3,2,1,0:T(8,128)(2,1)}), bf16[32,1,2,32,128]{4,3,2,1,0:T(8,128)(2,1)}, u32[]{:S(2)}, u32[]{:S(2)}) %all-to-all-start.3) | async-done | bytes 524320 | tf_op jit(solution)/shard_map/all_to_all | solution.py:114
  103.7 3.6 %all-to-all-start.2 = ((bf16[32,1,2,32,128]{4,3,2,1,0:T(8,128)(2,1)}), bf16[32,1,2,32,128]{4,3,2,1,0:T(8,128)(2,1)}, u32[]{:S(2)}, u32[]{:S(2)}) async-start(bf16[32,1,2,32,128]{4,3,2,1,0:T(8,128)(2,1)} %copy.108), calls=%async_computation.2 | async-start | bytes 1048576 | tf_op jit(solution)/shard_map/all_to_all | solution.py:114
  111.8 10.8 %all-to-all-done.2 = bf16[32,1,2,32,128]{4,3,2,1,0:T(8,128)(2,1)} async-done(((bf16[32,1,2,32,128]{4,3,2,1,0:T(8,128)(2,1)}), bf16[32,1,2,32,128]{4,3,2,1,0:T(8,128)(2,1)}, u32[]{:S(2)}, u32[]{:S(2)}) %all-to-all-start.2) | async-done | bytes 524320 | tf_op jit(solution)/shard_map/all_to_all | solution.py:114
  124.7 3.7 %fusion.34 = f32[8,64,513]{2,1,0:T(8,128)S(1)} fusion(bf16[8,513,512]{2,1,0:T(8,128)(2,1)} %fusion.18, bf16[8,64,128]{2,1,0:T(8,128)(2,1)S(1)} %bitcast.143, bf16[8,64,128]{2,1,0:T(8,128)(2,1)S(1)} %bitcast.144, bf16[8,64,128]{2,1,0:T(8,128)(2,1)S(1)} %bitcast.145, bf16[8,64,128]{2,1,0:T(8,128)(2,1)S(1)} %bitcast.142), kind=kOutput, calls=%fused_computation.45 | convolution fusion | flops 271056896 | bytes 5777408 | tf_op jit(solution)/shard_map/smo,sjo->smj/dot_general | solution.py:120
  132.2 3.4 %all-to-all-start.4 = ((bf16[8,1,2,8,2,513]{5,4,3,2,1,0:T(2,128)(2,1)}), bf16[8,1,2,8,2,513]{5,4,3,2,1,0:T(2,128)(2,1)S(1)}, u32[]{:S(2)}, u32[]{:S(2)}) async-start(bf16[8,1,2,8,2,513]{5,4,3,2,1,0:T(2,128)(2,1)} %copy_bitcast_fusion.6), calls=%async_computation.4 | async-start | bytes 655360 | tf_op jit(solution)/shard_map/all_to_all | solution.py:134
  135.6 3.7 %pad_maximum_fusion = bf16[1,192,2,1536]{3,2,1,0:T(2,128)(2,1)} fusion(bf16[1,192,1,1536]{3,2,1,0:T(2,128)(2,1)S(1)} %copy.107, bf16[1,192,1,1536]{3,2,1,0:T(2,128)(2,1)S(1)} %copy.106), kind=kLoop, calls=%fused_computation.34 | loop fusion | flops 2359296 | bytes 2359296 | tf_op jit(solution)/shard_map/stack | solution.py:123
  139.3 3.9 %all-to-all-done.4 = bf16[8,1,2,8,2,513]{5,4,3,2,1,0:T(2,128)(2,1)S(1)} async-done(((bf16[8,1,2,8,2,513]{5,4,3,2,1,0:T(2,128)(2,1)}), bf16[8,1,2,8,2,513]{5,4,3,2,1,0:T(2,128)(2,1)S(1)}, u32[]{:S(2)}, u32[]{:S(2)}) %all-to-all-start.4) | async-done | bytes 262688 | tf_op jit(solution)/shard_map/all_to_all | solution.py:134
  (73 shorter events, 24.9 us)
Async XLA Ops:
  2.9 14.6 %all-to-all-start = ((bf16[64,1,3,2,513]{4,3,2,1,0:T(2,128)(2,1)}), bf16[64,1,3,2,513]{4,3,2,1,0:T(2,128)(2,1)S(1)}, u32[]{:S(2)}, u32[]{:S(2)}) async-start(bf16[64,1,3,2,513]{4,3,2,1,0:T(2,128)(2,1)} %bitcast.125), calls=%async_computation | async-start | bytes 983040 | tf_op jit(solution)/shard_map/all_to_all | solution.py:85
  27.5 8.3 %copy-start.6 = (s32[256]{0:T(256)S(1)}, s32[256]{0:T(256)}, u32[]{:S(2)}) copy-start(s32[256]{0:T(256)} %param.6) | copy-start | bytes 3076
  29.6 43.8 %all-to-all-start.1 = ((bf16[32,1,3,2,32,128]{5,4,3,2,1,0:T(8,128)(2,1)}), bf16[32,1,3,2,32,128]{5,4,3,2,1,0:T(8,128)(2,1)}, u32[]{:S(2)}, u32[]{:S(2)}) async-start(bf16[32,1,3,2,32,128]{5,4,3,2,1,0:T(8,128)(2,1)} %bitcast.12), calls=%async_computation.1 | async-start | bytes 3145728 | tf_op jit(solution)/shard_map/all_to_all | solution.py:100
  53.1 1.7 %copy-start = (bf16[256,2,2,1536]{3,2,1,0:T(2,128)(2,1)}, bf16[256,2,2,1536]{3,2,1,0:T(2,128)(2,1)S(1)}, u32[]{:S(2)}) copy-start(bf16[256,2,2,1536]{3,2,1,0:T(2,128)(2,1)S(1)} %copy.102) | copy-start | bytes 9437188
  78.2 4.1 %copy-start.1 = (f32[1,2,2,128,1536]{4,3,2,1,0:T(8,128)}, f32[1,2,2,128,1536]{4,3,2,1,0:T(8,128)S(1)}, u32[]{:S(2)}) copy-start(f32[1,2,2,128,1536]{4,3,2,1,0:T(8,128)S(1)} %convolution_bitcast_fusion) | copy-start | bytes 9437188
  79.7 2.6 %copy-start.3 = (bf16[32,32,1536,1]{2,1,0,3:T(8,128)(2,1)S(1)}, bf16[32,32,1536,1]{2,1,0,3:T(8,128)(2,1)}, u32[]{:S(2)}) copy-start(bf16[32,32,1536,1]{2,1,0,3:T(8,128)(2,1)} %reshape.667) | copy-start | bytes 9437188
  82.4 1.0 copy-start.4
  84.3 19.4 %all-to-all-start.3 = ((bf16[32,1,2,32,128]{4,3,2,1,0:T(8,128)(2,1)}), bf16[32,1,2,32,128]{4,3,2,1,0:T(8,128)(2,1)}, u32[]{:S(2)}, u32[]{:S(2)}) async-start(bf16[32,1,2,32,128]{4,3,2,1,0:T(8,128)(2,1)} %copy.111), calls=%async_computation.3 | async-start | bytes 1048576 | tf_op jit(solution)/shard_map/all_to_all | solution.py:114
  88.3 19.3 %copy-start.2 = (f32[1,2,2,128,1536]{4,3,2,1,0:T(8,128)S(1)}, f32[1,2,2,128,1536]{4,3,2,1,0:T(8,128)}, u32[]{:S(2)}) copy-start(f32[1,2,2,128,1536]{4,3,2,1,0:T(8,128)} %copy-done.1) | copy-start | bytes 9437188
  103.7 18.9 %all-to-all-start.2 = ((bf16[32,1,2,32,128]{4,3,2,1,0:T(8,128)(2,1)}), bf16[32,1,2,32,128]{4,3,2,1,0:T(8,128)(2,1)}, u32[]{:S(2)}, u32[]{:S(2)}) async-start(bf16[32,1,2,32,128]{4,3,2,1,0:T(8,128)(2,1)} %copy.108), calls=%async_computation.2 | async-start | bytes 1048576 | tf_op jit(solution)/shard_map/all_to_all | solution.py:114
  107.6 1.2 copy-start.5
  107.9 20.5 %slice-start = ((s8[4259840]{0:T(1024)(128)(4,1)}), s8[65536]{0:T(1024)(128)(4,1)S(1)}, s32[]{:S(2)}) async-start(s8[4259840]{0:T(1024)(128)(4,1)} %bitcast.126), calls=%async_computation.5 | async-start | bytes 131072
  122.6 5.8 %slice-start.1 = ((s8[4259840]{0:T(1024)(128)(4,1)}), s8[4194304]{0:T(1024)(128)(4,1)S(1)}, s32[]{:S(2)}) async-start(s8[4259840]{0:T(1024)(128)(4,1)} %bitcast.126), calls=%async_computation.6 | async-start | bytes 8388608
  132.2 11.0 %all-to-all-start.4 = ((bf16[8,1,2,8,2,513]{5,4,3,2,1,0:T(2,128)(2,1)}), bf16[8,1,2,8,2,513]{5,4,3,2,1,0:T(2,128)(2,1)S(1)}, u32[]{:S(2)}, u32[]{:S(2)}) async-start(bf16[8,1,2,8,2,513]{5,4,3,2,1,0:T(2,128)(2,1)} %copy_bitcast_fusion.6), calls=%async_computation.4 | async-start | bytes 655360 | tf_op jit(solution)/shard_map/all_to_all | solution.py:134
